TPU v7x, 512 devices: a whole 4x8x8 slice. The times are simulated.
512 devices in a mesh: pipe: 4 (over x), tm: 32 (over y_lo, z), dp: 4 (over y_hi, core).
Axes of the slice: x: 4, y: 8 (y_hi: 2, y_lo: 4; y = y_hi * 4 + y_lo), z: 8, core: 2. Of those that a mesh axis runs over, the one named last changes fastest.
Arguments:
- video: bfloat16 [4, 4, 64, 64, 320], P(None, 'dp', 'tm'), may hold values from -6 to 6
- cotangent: bfloat16 [4, 4, 64, 64, 320], P(None, 'dp', 'tm'), may hold values from -6 to 6
- timesteps: int32 [4, 4], P(None, 'dp'), may hold values from 0 to 999
- conv_weight: bfloat16 [4, 3, 320, 320], P('pipe'), may hold values from -0.1875 to 0.1875
- out_weight: bfloat16 [4, 320, 320], P('pipe'), may hold values from -0.3125 to 0.3125
Outputs:
- conv_grad: float32 [4, 3, 320, 320], P('pipe')
- out_grad: float32 [4, 320, 320], P('pipe')
All inputs are finite; a program needn't handle non-finite values.
Results may differ from a plain program's by a relative error of at most 0.012.
Values may be sent and summed in bfloat16 or wider, within the bound.
A program may use at most 64 MiB of HBM per device.

v0:
```python
import math
import jax
import jax.numpy as jnp
from jax import lax
from jax.sharding import PartitionSpec as P

EPSILON = 1e-06


def padded_2(block, sides, width):
    for axis, dim in sides:
        count = lax.axis_size(axis)
        forward = [(i, i + 1) for i in range(count - 1)]
        backward = [(target, source) for source, target in forward]
        low = lax.ppermute(
            lax.slice_in_dim(block, block.shape[dim] - width, None, axis=dim), axis, forward
        )
        high = lax.ppermute(lax.slice_in_dim(block, 0, width, axis=dim), axis, backward)
        block = jnp.concatenate([low, block, high], axis=dim)
    return block


def from_partner(value, axis, stride):
    mask = 2**stride
    pairs = [(source, source ^ mask) for source in range(lax.axis_size(axis))]
    return lax.ppermute(value, axis, pairs)


def from_behind(array, axis, by):
    peers = lax.axis_size(axis)
    pairs = [(i, i + by) for i in range(peers) if 0 <= i + by < peers]
    return lax.ppermute(array, axis, pairs)


def embed(times, channels):
    half = channels // 2
    index = jnp.arange(half).astype(jnp.float32)
    freq = jnp.exp(index * (-math.log(10000.0) / half))
    angle = times.astype(jnp.float32)[..., None] * freq
    return jnp.concatenate([jnp.sin(angle), jnp.cos(angle)], -1)


def prepare(inputs, emb_pair, conv_pair):
    x_float = inputs.astype(jnp.float32)
    inv_rms = lax.rsqrt(jnp.mean(x_float * x_float, -1, keepdims=True) + EPSILON)
    normed = x_float * inv_rms
    norm_low = normed.astype(jnp.bfloat16)
    padded = padded_2(norm_low, (("tm", 1),), 1)
    frames = inputs.shape[1]
    pre_act = emb_pair[:, None, None, :]
    for offset in range(3):
        pre_act = pre_act + jnp.einsum(
            "dfpc,dcx->dfpx",
            padded[:, offset : offset + frames],
            conv_pair[:, offset],
            preferred_element_type=jnp.float32,
        )
    active = jax.nn.silu(pre_act).astype(jnp.bfloat16)
    return (inv_rms, normed, padded, pre_act, active)


def body(video, cotangent, timesteps, conv_weight, out_weight):
    current_section_index = lax.axis_index("pipe")
    sections = lax.axis_size("pipe")
    final_section = sections - 1
    micro = video.shape[0]
    half_microbatch_count = micro // 2
    ticks = half_microbatch_count + sections - 1
    channels = video.shape[-1]
    frames = video.shape[2]
    bit_count = sections.bit_length() - 1
    packed = jnp.concatenate([conv_weight[0], out_weight[0][None]], 0)
    mirrored = packed
    for bit_pos in range(bit_count):
        mirrored = from_partner(mirrored, "pipe", bit_pos)
    conv_pair = jnp.stack([conv_weight[0], mirrored[:3]])
    out_pair = jnp.stack([out_weight[0], mirrored[3]])
    embedded = embed(timesteps[:, 0], channels)

    def pick(stacked, down_tick, up_tick):
        down_part = lax.dynamic_index_in_dim(
            stacked, jnp.clip(down_tick, 0, ticks - 1), 0, keepdims=False
        )[0]
        up_part = lax.dynamic_index_in_dim(
            stacked, jnp.clip(up_tick, 0, ticks - 1), 0, keepdims=False
        )[1]
        return jnp.stack([down_part, up_part])

    empty_activation = jnp.zeros(video.shape[2:], jnp.bfloat16)
    down_buf = empty_activation
    up_buf = empty_activation
    saved = []
    for current_clock_tick in range(ticks):
        down_in = down_buf
        up_in = up_buf
        if current_clock_tick < half_microbatch_count:
            down_in = jnp.where(current_section_index == 0, video[current_clock_tick, 0], down_buf)
            up_in = jnp.where(
                current_section_index == final_section,
                video[half_microbatch_count + current_clock_tick, 0],
                up_buf,
            )
        inputs = jnp.stack([down_in, up_in])
        down_row = lax.dynamic_index_in_dim(
            embedded,
            jnp.clip(current_clock_tick - current_section_index, 0, half_microbatch_count - 1),
            0,
            keepdims=False,
        )
        up_row = lax.dynamic_index_in_dim(
            embedded,
            half_microbatch_count
            + jnp.clip(
                current_clock_tick - (final_section - current_section_index),
                0,
                half_microbatch_count - 1,
            ),
            0,
            keepdims=False,
        )
        emb_pair = jnp.stack([down_row, up_row])
        inv_rms, normed, padded, pre_act, active = prepare(inputs, emb_pair, conv_pair)
        outputs = (
            inputs.astype(jnp.float32)
            + jnp.einsum("dfpc,dcx->dfpx", active, out_pair, preferred_element_type=jnp.float32)
        ).astype(jnp.bfloat16)
        saved.append((inv_rms, normed, padded, pre_act, active))
        if current_clock_tick + 1 < ticks:
            down_buf = from_behind(outputs[0], "pipe", 1)
            up_buf = from_behind(outputs[1], "pipe", -1)
    stored = jax.tree.map(lambda *leaves: jnp.stack(leaves), *saved)
    conv_acc = jnp.zeros((2, 3, channels, channels), jnp.float32)
    out_acc = jnp.zeros((2, channels, channels), jnp.float32)
    downward_gradient_holder = empty_activation
    upward_gradient_holder = empty_activation
    for current_clock_tick in range(ticks):
        down_micro = current_clock_tick - (final_section - current_section_index)
        up_micro = current_clock_tick - current_section_index
        down_valid = (down_micro >= 0) & (down_micro < half_microbatch_count)
        up_valid = (up_micro >= 0) & (up_micro < half_microbatch_count)
        downward_hidden_gradient = downward_gradient_holder
        upward_hidden_gradient = upward_gradient_holder
        if current_clock_tick < half_microbatch_count:
            downward_hidden_gradient = jnp.where(
                current_section_index == final_section,
                cotangent[current_clock_tick, 0],
                downward_gradient_holder,
            )
            upward_hidden_gradient = jnp.where(
                current_section_index == 0,
                cotangent[half_microbatch_count + current_clock_tick, 0],
                upward_gradient_holder,
            )
        downward_hidden_gradient = jnp.where(down_valid, downward_hidden_gradient, empty_activation)
        upward_hidden_gradient = jnp.where(up_valid, upward_hidden_gradient, empty_activation)
        grad_out = jnp.stack([downward_hidden_gradient, upward_hidden_gradient])
        down_tick = down_micro + current_section_index
        up_tick = up_micro + final_section - current_section_index
        inv_rms, normed, padded, pre_act, active = tuple(
            (pick(item, down_tick, up_tick) for item in stored)
        )
        out_acc = out_acc + jnp.einsum(
            "dfpc,dfpx->dcx", active, grad_out, preferred_element_type=jnp.float32
        )
        grad_act = jnp.einsum(
            "dfpx,dcx->dfpc", grad_out, out_pair, preferred_element_type=jnp.float32
        )
        sigma = jax.nn.sigmoid(pre_act)
        grad_pre = (grad_act * sigma * (1.0 + pre_act * (1.0 - sigma))).astype(jnp.bfloat16)
        grad_pad = padded_2(grad_pre, (("tm", 1),), 1)
        conv_terms = []
        grad_norm = jnp.zeros(normed.shape, jnp.float32)
        for offset in range(3):
            conv_terms.append(
                jnp.einsum(
                    "dfpc,dfpx->dcx",
                    padded[:, offset : offset + frames],
                    grad_pre,
                    preferred_element_type=jnp.float32,
                )
            )
            grad_norm = grad_norm + jnp.einsum(
                "dfpx,dcx->dfpc",
                grad_pad[:, 2 - offset : 2 - offset + frames],
                conv_pair[:, offset],
                preferred_element_type=jnp.float32,
            )
        conv_acc = conv_acc + jnp.stack(conv_terms, 1)
        incoming_gradient = grad_out.astype(jnp.float32) + inv_rms * (
            grad_norm - normed * jnp.mean(grad_norm * normed, -1, keepdims=True)
        )
        incoming_gradient = incoming_gradient.astype(jnp.bfloat16)
        if current_clock_tick + 1 < ticks:
            downward_gradient_holder = from_behind(incoming_gradient[0], "pipe", -1)
            upward_gradient_holder = from_behind(incoming_gradient[1], "pipe", 1)
    down_total = jnp.concatenate([conv_acc[0], out_acc[0][None]], 0)
    up_total = jnp.concatenate([conv_acc[1], out_acc[1][None]], 0)
    down_sum, up_sum = lax.psum((down_total, up_total), ("tm", "dp"))
    value = up_sum
    for bit_pos in range(bit_count):
        value = from_partner(value.astype(jnp.bfloat16), "pipe", bit_pos).astype(value.dtype)
    total = down_sum + value
    row_count = (
        micro * video.shape[1] * lax.axis_size("dp") * frames * lax.axis_size("tm") * video.shape[3]
    )
    scale = 1.0 / math.sqrt(row_count)
    return ((total[:3] * scale)[None], (total[3] * scale)[None])


def solution(mesh):
    return jax.shard_map(
        body,
        mesh=mesh,
        in_specs=(
            P(None, "dp", "tm", None, None),
            P(None, "dp", "tm", None, None),
            P(None, "dp"),
            P("pipe", None, None, None),
            P("pipe", None, None),
        ),
        out_specs=(P("pipe", None, None, None), P("pipe", None, None)),
        check_vma=False,
    )
```

profile of v0, /device:TPU:24, one launch (start us, length us, event | category | flops | bytes accessed | tf_op | source)
XLA Modules:
  0.0 1158.5 jit_solution(2011999744393750065)
XLA Ops:
  8.5 10.8 collective-permute-start.1
  22.8 3.5 collective-permute-start.2
  26.7 21.4 %collective-permute-done.2 = bf16[4,320,320]{2,1,0:T(8,128)(2,1)} collective-permute-done((bf16[4,320,320]{2,1,0:T(8,128)(2,1)S(1)}, bf16[4,320,320]{2,1,0:T(8,128)(2,1)}, u32[]{:S(2)}, u32[]{:S(2)}) %collective-permute-start.2) | collective-permute-done | bytes 819232 | tf_op jit(solution)/shard_map/ppermute | solution.py:26
  48.1 4.9 collective-permute-start.3
  53.4 20.6 %collective-permute-done.3 = bf16[4,320,320]{2,1,0:T(8,128)(2,1)S(1)} collective-permute-done((bf16[4,320,320]{2,1,0:T(8,128)(2,1)}, bf16[4,320,320]{2,1,0:T(8,128)(2,1)S(1)}, u32[]{:S(2)}, u32[]{:S(2)}) %collective-permute-start.3) | collective-permute-done | bytes 819232 | tf_op jit(solution)/shard_map/ppermute | solution.py:26
  77.8 3.4 collective-permute-start.4
  83.4 4.3 collective-permute-done.5
  90.4 6.0 collective-permute-start.7
  99.4 3.4 collective-permute-start.8
  105.0 4.3 collective-permute-done.9
  111.9 6.4 collective-permute-start.11
  121.3 3.1 collective-permute-start.12
  126.6 4.3 collective-permute-done.13
  133.5 6.4 collective-permute-start.15
  147.0 4.3 collective-permute-done.17
  151.9 6.4 collective-permute-start.19
  160.6 6.3 collective-permute-done.18
  171.8 6.2 collective-permute-start.20
  181.9 4.6 collective-permute-start.23
  192.7 6.4 collective-permute-start.24
  203.6 4.9 collective-permute-start.27
  214.0 6.4 collective-permute-start.28
  225.3 5.2 collective-permute-start.31
  236.7 6.2 collective-permute-start.32
  247.7 5.0 collective-permute-start.35
  252.8 2.2 collective-permute-done.35
  259.1 641.5 %all-reduce.4 = bf16[4,320,320]{2,1,0:T(8,128)(2,1)} all-reduce(f32[4,320,320]{2,1,0:T(8,128)S(1)} %pad_maximum_fusion.1), channel_id=1, replica_groups=mesh['pipe'=4,'tm'=32,'dp'=4] {'tm','dp'}, use_global_device_ids=true, to_apply=%region_10.11 | all-reduce | flops 409600 | bytes 2457600 | tf_op jit(solution)/shard_map/psum | solution.py:198
  900.6 3.7 collective-permute-start.36
  904.3 2.5 pad_maximum_fusion
  906.8 12.7 %collective-permute-done.36 = bf16[4,320,320]{2,1,0:T(8,128)(2,1)S(1)} collective-permute-done((bf16[4,320,320]{2,1,0:T(8,128)(2,1)}, bf16[4,320,320]{2,1,0:T(8,128)(2,1)S(1)}, u32[]{:S(2)}, u32[]{:S(2)}) %collective-permute-start.36) | collective-permute-done | bytes 819232 | tf_op jit(solution)/shard_map/ppermute | solution.py:26
  919.5 10.0 collective-permute-start.37
  929.5 218.4 %all-reduce.3.cloned.1.call-done = f32[4,320,320]{2,1,0:T(8,128)} async-done(((f32[4,320,320]{2,1,0:T(8,128)}), f32[4,320,320]{2,1,0:T(8,128)}) %all-reduce.3.cloned.1.call-update) | async-done | bytes 1638416 | tf_op jit(solution)/shard_map/psum | solution.py:198
  (217 shorter events, 87.1 us)
Async XLA Ops:
  7.2 1140.7 %all-reduce.3.cloned.1.call-start = ((), (), s32[]{:S(2)}) async-start(), calls=%async_computation | async-start | bytes 3932160 | tf_op jit(solution)/shard_map/psum | solution.py:198
  8.5 44.8 %collective-permute-start.1 = (bf16[2,1,64,320]{3,2,1,0:T(8,128)(2,1)S(1)}, bf16[2,1,64,320]{3,2,1,0:T(8,128)(2,1)S(1)}, u32[]{:S(2)}, u32[]{:S(2)}) collective-permute-start(bf16[2,1,64,320]{3,2,1,0:T(8,128)(2,1)S(1)} %get-tuple-element.91), channel_id=1, source_target_pairs={{4,0},{8,4},{12,8},{16,12},{20,16},{24,20},{28,24},{32,28},{36,32}... | collective-permute-start | bytes 245768 | tf_op jit(solution)/shard_map/ppermute | solution.py:18
  19.4 34.0 %collective-permute-start = (bf16[2,1,64,320]{3,2,1,0:T(8,128)(2,1)S(1)}, bf16[2,1,64,320]{3,2,1,0:T(8,128)(2,1)S(1)}, u32[]{:S(2)}, u32[]{:S(2)}) collective-permute-start(bf16[2,1,64,320]{3,2,1,0:T(8,128)(2,1)S(1)} %get-tuple-element.92), channel_id=1, source_target_pairs={{0,4},{4,8},{8,12},{12,16},{16,20},{20,24},{24,28},{28,32},{32,36}... | collective-permute-start | bytes 245768 | tf_op jit(solution)/shard_map/ppermute | solution.py:15
  22.8 25.3 %collective-permute-start.2 = (bf16[4,320,320]{2,1,0:T(8,128)(2,1)S(1)}, bf16[4,320,320]{2,1,0:T(8,128)(2,1)}, u32[]{:S(2)}, u32[]{:S(2)}) collective-permute-start(bf16[4,320,320]{2,1,0:T(8,128)(2,1)S(1)} %pad_maximum_fusion.2), channel_id=1, source_target_pairs={{0,128},{128,0},{256,384},{384,256},{1,129},{129,1},{257,385},{385... | collective-permute-start | bytes 2457608 | tf_op jit(solution)/shard_map/ppermute | solution.py:26
  48.1 25.9 %collective-permute-start.3 = (bf16[4,320,320]{2,1,0:T(8,128)(2,1)}, bf16[4,320,320]{2,1,0:T(8,128)(2,1)S(1)}, u32[]{:S(2)}, u32[]{:S(2)}) collective-permute-start(bf16[4,320,320]{2,1,0:T(8,128)(2,1)} %collective-permute-done.2), channel_id=1, source_target_pairs={{0,256},{128,384},{256,0},{384,128},{1,257},{129,385},{257,1},{385... | collective-permute-start | bytes 2457608 | tf_op jit(solution)/shard_map/ppermute | solution.py:26
  81.2 6.5 collective-permute-start.5
  88.4 8.6 collective-permute-start.6
  90.4 8.2 collective-permute-start.7
  102.8 6.5 collective-permute-start.9
  109.9 9.0 collective-permute-start.10
  111.9 8.6 collective-permute-start.11
  131.5 9.0 collective-permute-start.14
  133.5 8.6 collective-permute-start.15
  151.9 15.3 %collective-permute-start.19 = (bf16[2,1,64,320]{3,2,1,0:T(8,128)(2,1)S(1)}, bf16[2,1,64,320]{3,2,1,0:T(8,128)(2,1)S(1)}, u32[]{:S(2)}, u32[]{:S(2)}) collective-permute-start(bf16[2,1,64,320]{3,2,1,0:T(8,128)(2,1)S(1)} %get-tuple-element.75), channel_id=1, source_target_pairs={{4,0},{8,4},{12,8},{16,12},{20,16},{24,20},{28,24},{32,28},{36,32}... | collective-permute-start | bytes 245768 | tf_op jit(solution)/shard_map/ppermute | solution.py:18
  158.3 8.6 collective-permute-start.18
  169.6 8.6 collective-permute-start.21
  171.8 8.2 collective-permute-start.20
  181.9 6.8 collective-permute-start.23
  189.8 9.4 collective-permute-start.25
  192.7 8.6 collective-permute-start.24
  201.9 6.9 collective-permute-start.26
  203.6 7.1 collective-permute-start.27
  211.8 9.2 collective-permute-start.29
  214.0 9.1 collective-permute-start.28
  223.7 7.9 collective-permute-start.30
  225.3 8.1 collective-permute-start.31
  234.5 8.8 collective-permute-start.33
  236.7 8.4 collective-permute-start.32
  245.8 7.0 collective-permute-start.34
  247.7 7.2 collective-permute-start.35
  900.6 18.9 %collective-permute-start.36 = (bf16[4,320,320]{2,1,0:T(8,128)(2,1)}, bf16[4,320,320]{2,1,0:T(8,128)(2,1)S(1)}, u32[]{:S(2)}, u32[]{:S(2)}) collective-permute-start(bf16[4,320,320]{2,1,0:T(8,128)(2,1)} %all-reduce.4), channel_id=1, source_target_pairs={{0,128},{128,0},{256,384},{384,256},{1,129},{129,1},{257,385},{385... | collective-permute-start | bytes 2457608 | tf_op jit(solution)/shard_map/ppermute | solution.py:26
  919.5 228.5 %collective-permute-start.37 = (bf16[4,320,320]{2,1,0:T(8,128)(2,1)S(1)}, bf16[4,320,320]{2,1,0:T(8,128)(2,1)S(1)}, u32[]{:S(2)}, u32[]{:S(2)}) collective-permute-start(bf16[4,320,320]{2,1,0:T(8,128)(2,1)S(1)} %collective-permute-done.36), channel_id=1, source_target_pairs={{0,256},{128,384},{256,0},{384,128},{1,257},{129,385},{257,1},{385... | collective-permute-start | bytes 2457608 | tf_op jit(solution)/shard_map/ppermute | solution.py:26
  (13 other events, 169.7 us)
Sparse Core Ops, SparseCore 0:
  906.9 240.9 all-reduce.2
where the time goes:
time: 1160 us
  blocking collectives  641 us (55%)
  waiting for transfers between devices  323 us (28%)
  starting transfers between devices  143 us (12%)
  matrix products  18.2 us (2%)
  between operations  15.5 us (1%)
  other arithmetic  13.4 us (1%)
    psum x1, blocking collectives, body(): down_sum, up_sum = lax.psum((down_total, up_total), ('tm', 'dp'))  641 us
    psum x1, waiting for transfers between devices, body(): down_sum, up_sum = lax.psum((down_total, up_total), ('tm', 'dp'))  218 us
    ppermute x9, starting transfers between devices, padded_2(): lax.ppermute(lax.slice_in_dim(block, 0, width, axis=dim), axis, backward)  61.4 us
    ppermute x4, waiting for transfers between devices, from_partner(): return lax.ppermute(value, axis, pairs)  54.6 us
    ppermute x16, starting transfers between devices, from_behind(): return lax.ppermute(array, axis, pairs)  41.9 us
    ppermute x16, waiting for transfers between devices, from_behind(): return lax.ppermute(array, axis, pairs)  29.7 us
  transfers between devices with their start and end apart: 39, of which 33 were waited for; matrix products, arithmetic and copies ran while one was open for 1% of the time, Pallas kernels for 0%

commit v1 on v0

--- a/solution.py
+++ b/solution.py
@@ -195,7 +195,7 @@
             upward_gradient_holder = from_behind(incoming_gradient[1], "pipe", 1)
     down_total = jnp.concatenate([conv_acc[0], out_acc[0][None]], 0)
     up_total = jnp.concatenate([conv_acc[1], out_acc[1][None]], 0)
-    down_sum, up_sum = lax.psum((down_total, up_total), ("tm", "dp"))
+    down_sum, up_sum = lax.psum(lax.psum((down_total, up_total), "dp"), "tm")
     value = up_sum
     for bit_pos in range(bit_count):
         value = from_partner(value.astype(jnp.bfloat16), "pipe", bit_pos).astype(value.dtype)

time: 1160 us -> 751 us (0.65)
  the two profiles are of different devices: /device:TPU:24 before, /device:TPU:2 now
where the time goes in v1:
time: 751 us; the launch traced here: 750 us
  waiting for transfers between devices  401 us (53%)
  blocking collectives  179 us (24%)
  starting transfers between devices  119 us (16%)
  matrix products  18.3 us (2%)
  between operations  15.5 us (2%)
  other arithmetic  13.1 us (2%)
    psum x2, waiting for transfers between devices, body(): down_sum, up_sum = lax.psum(lax.psum((down_total, up_total), 'dp'), 'tm')  279 us
    psum x1, blocking collectives, body(): down_sum, up_sum = lax.psum(lax.psum((down_total, up_total), 'dp'), 'tm')  179 us
    ppermute x4, waiting for transfers between devices, from_partner(): return lax.ppermute(value, axis, pairs)  56.8 us
    ppermute x16, starting transfers between devices, from_behind(): return lax.ppermute(array, axis, pairs)  47.9 us
    ppermute x9, starting transfers between devices, padded_2(): lax.ppermute(lax.slice_in_dim(block, block.shape[dim] - width, None, axis...  41 us
    ppermute x9, waiting for transfers between devices, padded_2(): lax.ppermute(lax.slice_in_dim(block, 0, width, axis=dim), axis, backward)  33.3 us
    ppermute x16, waiting for transfers between devices, from_behind(): return lax.ppermute(array, axis, pairs)  25.2 us
    ppermute x4, starting transfers between devices, from_partner(): return lax.ppermute(value, axis, pairs)  18.7 us
  transfers between devices with their start and end apart: 40, of which 34 were waited for; matrix products, arithmetic and copies ran while one was open for 1% of the time, Pallas kernels for 0%

profile of v1, /device:TPU:2, one launch (start us, length us, event | category | flops | bytes accessed | tf_op | source)
XLA Modules:
  0.0 749.6 jit_solution(101696589367787998)
XLA Ops:
  9.8 4.9 collective-permute-start
  16.2 7.6 %collective-permute-start.2 = (bf16[4,320,320]{2,1,0:T(8,128)(2,1)S(1)}, bf16[4,320,320]{2,1,0:T(8,128)(2,1)}, u32[]{:S(2)}, u32[]{:S(2)}) collective-permute-start(bf16[4,320,320]{2,1,0:T(8,128)(2,1)S(1)} %pad_maximum_fusion.2), channel_id=1, source_target_pairs={{0,128},{128,0},{256,384},{384,256},{1,129},{129,1},{257,385},{385... | collective-permute-start | bytes 2457608 | tf_op jit(solution)/shard_map/ppermute | solution.py:26
  24.2 17.3 %collective-permute-done.2 = bf16[4,320,320]{2,1,0:T(8,128)(2,1)} collective-permute-done((bf16[4,320,320]{2,1,0:T(8,128)(2,1)S(1)}, bf16[4,320,320]{2,1,0:T(8,128)(2,1)}, u32[]{:S(2)}, u32[]{:S(2)}) %collective-permute-start.2) | collective-permute-done | bytes 819232 | tf_op jit(solution)/shard_map/ppermute | solution.py:26
  41.5 4.0 collective-permute-start.3
  46.0 20.4 %collective-permute-done.3 = bf16[4,320,320]{2,1,0:T(8,128)(2,1)S(1)} collective-permute-done((bf16[4,320,320]{2,1,0:T(8,128)(2,1)}, bf16[4,320,320]{2,1,0:T(8,128)(2,1)S(1)}, u32[]{:S(2)}, u32[]{:S(2)}) %collective-permute-start.3) | collective-permute-done | bytes 819232 | tf_op jit(solution)/shard_map/ppermute | solution.py:26
  68.4 4.5 collective-permute-start.4
  75.1 4.3 collective-permute-done.5
  80.0 4.3 collective-permute-start.6
  86.8 4.5 collective-permute-done.7
  102.2 5.5 collective-permute-start.10
  110.2 4.2 collective-permute-done.11
  117.0 3.9 collective-permute-start.13
  124.1 4.6 collective-permute-start.14
  131.2 4.2 collective-permute-done.15
  138.0 3.9 collective-permute-start.17
  146.4 4.6 collective-permute-start.18
  155.7 4.3 collective-permute-start.21
  162.5 4.4 collective-permute-done.20
  174.1 3.9 collective-permute-done.23
  179.1 5.1 collective-permute-start.25
  186.8 6.5 collective-permute-done.24
  196.2 3.9 collective-permute-start.27
  203.8 5.9 collective-permute-start.29
  212.3 5.0 collective-permute-done.28
  220.2 4.4 collective-permute-start.31
  232.6 4.6 collective-permute-done.32
  240.5 4.0 collective-permute-start.35
  252.6 165.1 %all-reduce.7.cloned.1.call-done = (f32[4,320,320]{2,1,0:T(8,128)}, f32[4,320,320]{2,1,0:T(8,128)}) async-done(((f32[4,320,320]{2,1,0:T(8,128)}, f32[4,320,320]{2,1,0:T(8,128)}), (f32[4,320,320]{2,1,0:T(8,128)}, f32[4,320,320]{2,1,0:T(8,128)})) %all-reduce.7.cloned.1.call-update) | async-done | bytes 3276816 | tf_op jit(solution)/shard_map/psum | solution.py:198
  419.3 179.2 %all-reduce.8 = bf16[4,320,320]{2,1,0:T(8,128)(2,1)S(1)} all-reduce(f32[4,320,320]{2,1,0:T(8,128)S(1)} %copy-done.1), channel_id=1, replica_groups=mesh['pipe'=4,'tm'=32,'dp'=4] {'tm'}, use_global_device_ids=true, to_apply=%region_12.13 | all-reduce | flops 409600 | bytes 2457600 | tf_op jit(solution)/shard_map/psum | solution.py:198
  601.0 19.2 %collective-permute-done.36 = bf16[4,320,320]{2,1,0:T(8,128)(2,1)S(1)} collective-permute-done((bf16[4,320,320]{2,1,0:T(8,128)(2,1)S(1)}, bf16[4,320,320]{2,1,0:T(8,128)(2,1)S(1)}, u32[]{:S(2)}, u32[]{:S(2)}) %collective-permute-start.36) | collective-permute-done | bytes 819232 | tf_op jit(solution)/shard_map/ppermute | solution.py:26
  620.2 4.5 collective-permute-start.37
  624.7 114.3 %all-reduce.5.cloned.1.call-done = f32[4,320,320]{2,1,0:T(8,128)} async-done(((f32[4,320,320]{2,1,0:T(8,128)}), f32[4,320,320]{2,1,0:T(8,128)}) %all-reduce.5.cloned.1.call-update) | async-done | bytes 1638416 | tf_op jit(solution)/shard_map/psum | solution.py:198
  (219 shorter events, 97.2 us)
Async XLA Ops:
  7.2 410.5 %all-reduce.7.cloned.1.call-start = ((), (), s32[]{:S(2)}) async-start(), calls=%async_computation.1 | async-start | bytes 7864320 | tf_op jit(solution)/shard_map/psum | solution.py:198
  8.5 37.4 %collective-permute-start.1 = (bf16[2,1,64,320]{3,2,1,0:T(8,128)(2,1)S(1)}, bf16[2,1,64,320]{3,2,1,0:T(8,128)(2,1)S(1)}, u32[]{:S(2)}, u32[]{:S(2)}) collective-permute-start(bf16[2,1,64,320]{3,2,1,0:T(8,128)(2,1)S(1)} %get-tuple-element.93), channel_id=1, source_target_pairs={{4,0},{8,4},{12,8},{16,12},{20,16},{24,20},{28,24},{32,28},{36,32}... | collective-permute-start | bytes 245768 | tf_op jit(solution)/shard_map/ppermute | solution.py:18
  9.8 36.1 %collective-permute-start = (bf16[2,1,64,320]{3,2,1,0:T(8,128)(2,1)S(1)}, bf16[2,1,64,320]{3,2,1,0:T(8,128)(2,1)S(1)}, u32[]{:S(2)}, u32[]{:S(2)}) collective-permute-start(bf16[2,1,64,320]{3,2,1,0:T(8,128)(2,1)S(1)} %get-tuple-element.94), channel_id=1, source_target_pairs={{0,4},{4,8},{8,12},{12,16},{16,20},{20,24},{24,28},{28,32},{32,36}... | collective-permute-start | bytes 245768 | tf_op jit(solution)/shard_map/ppermute | solution.py:15
  16.2 25.3 %collective-permute-start.2 = (bf16[4,320,320]{2,1,0:T(8,128)(2,1)S(1)}, bf16[4,320,320]{2,1,0:T(8,128)(2,1)}, u32[]{:S(2)}, u32[]{:S(2)}) collective-permute-start(bf16[4,320,320]{2,1,0:T(8,128)(2,1)S(1)} %pad_maximum_fusion.2), channel_id=1, source_target_pairs={{0,128},{128,0},{256,384},{384,256},{1,129},{129,1},{257,385},{385... | collective-permute-start | bytes 2457608 | tf_op jit(solution)/shard_map/ppermute | solution.py:26
  41.5 24.8 %collective-permute-start.3 = (bf16[4,320,320]{2,1,0:T(8,128)(2,1)}, bf16[4,320,320]{2,1,0:T(8,128)(2,1)S(1)}, u32[]{:S(2)}, u32[]{:S(2)}) collective-permute-start(bf16[4,320,320]{2,1,0:T(8,128)(2,1)} %collective-permute-done.2), channel_id=1, source_target_pairs={{0,256},{128,384},{256,0},{384,128},{1,257},{129,385},{257,1},{385... | collective-permute-start | bytes 2457608 | tf_op jit(solution)/shard_map/ppermute | solution.py:26
  68.4 6.7 collective-permute-start.4
  72.9 6.5 collective-permute-start.5
  84.4 6.9 collective-permute-start.7
  92.0 6.5 collective-permute-start.8
  95.1 6.5 collective-permute-start.9
  102.2 7.7 %collective-permute-start.10 = (bf16[2,1,64,320]{3,2,1,0:T(8,128)(2,1)S(1)}, bf16[2,1,64,320]{3,2,1,0:T(8,128)(2,1)S(1)}, u32[]{:S(2)}, u32[]{:S(2)}) collective-permute-start(bf16[2,1,64,320]{3,2,1,0:T(8,128)(2,1)S(1)} %get-tuple-element.86), channel_id=1, source_target_pairs={{0,4},{4,8},{8,12},{12,16},{16,20},{20,24},{24,28},{28,32},{32,36}... | collective-permute-start | bytes 245768 | tf_op jit(solution)/shard_map/ppermute | solution.py:15
  107.9 6.5 collective-permute-start.11
  117.0 6.5 collective-permute-start.13
  124.1 6.8 collective-permute-start.14
  128.8 6.5 collective-permute-start.15
  145.1 8.3 %collective-permute-start.19 = (bf16[2,1,64,320]{3,2,1,0:T(8,128)(2,1)S(1)}, bf16[2,1,64,320]{3,2,1,0:T(8,128)(2,1)S(1)}, u32[]{:S(2)}, u32[]{:S(2)}) collective-permute-start(bf16[2,1,64,320]{3,2,1,0:T(8,128)(2,1)S(1)} %get-tuple-element.77), channel_id=1, source_target_pairs={{4,0},{8,4},{12,8},{16,12},{20,16},{24,20},{28,24},{32,28},{36,32}... | collective-permute-start | bytes 245768 | tf_op jit(solution)/shard_map/ppermute | solution.py:18
  146.4 6.8 collective-permute-start.18
  155.7 6.5 collective-permute-start.21
  160.3 6.6 collective-permute-start.20
  171.5 6.5 collective-permute-start.23
  179.1 7.4 collective-permute-start.25
  185.2 8.1 %collective-permute-start.24 = (bf16[2,1,64,320]{3,2,1,0:T(8,128)(2,1)S(1)}, bf16[2,1,64,320]{3,2,1,0:T(8,128)(2,1)S(1)}, u32[]{:S(2)}, u32[]{:S(2)}) collective-permute-start(bf16[2,1,64,320]{3,2,1,0:T(8,128)(2,1)S(1)} %get-tuple-element.71), channel_id=1, source_target_pairs={{4,0},{8,4},{12,8},{16,12},{20,16},{24,20},{28,24},{32,28},{36,32}... | collective-permute-start | bytes 245768 | tf_op jit(solution)/shard_map/ppermute | solution.py:18
  193.9 6.5 collective-permute-start.26
  203.8 8.2 %collective-permute-start.29 = (bf16[2,1,64,320]{3,2,1,0:T(8,128)(2,1)S(1)}, bf16[2,1,64,320]{3,2,1,0:T(8,128)(2,1)S(1)}, u32[]{:S(2)}, u32[]{:S(2)}) collective-permute-start(bf16[2,1,64,320]{3,2,1,0:T(8,128)(2,1)S(1)} %get-tuple-element.68), channel_id=1, source_target_pairs={{0,4},{4,8},{8,12},{12,16},{16,20},{20,24},{24,28},{28,32},{32,36}... | collective-permute-start | bytes 245768 | tf_op jit(solution)/shard_map/ppermute | solution.py:15
  210.0 7.3 collective-permute-start.28
  217.9 7.3 collective-permute-start.30
  220.2 7.1 collective-permute-start.31
  230.5 6.8 collective-permute-start.32
  237.9 6.6 collective-permute-start.34
  252.6 486.5 %all-reduce.5.cloned.1.call-start = ((), (), s32[]{:S(2)}) async-start(), calls=%async_computation | async-start | bytes 3932160 | tf_op jit(solution)/shard_map/psum | solution.py:198
  598.4 21.7 %collective-permute-start.36 = (bf16[4,320,320]{2,1,0:T(8,128)(2,1)S(1)}, bf16[4,320,320]{2,1,0:T(8,128)(2,1)S(1)}, u32[]{:S(2)}, u32[]{:S(2)}) collective-permute-start(bf16[4,320,320]{2,1,0:T(8,128)(2,1)S(1)} %all-reduce.8), channel_id=1, source_target_pairs={{0,128},{128,0},{256,384},{384,256},{1,129},{129,1},{257,385},{385... | collective-permute-start | bytes 2457608 | tf_op jit(solution)/shard_map/ppermute | solution.py:26
  620.2 118.9 %collective-permute-start.37 = (bf16[4,320,320]{2,1,0:T(8,128)(2,1)S(1)}, bf16[4,320,320]{2,1,0:T(8,128)(2,1)S(1)}, u32[]{:S(2)}, u32[]{:S(2)}) collective-permute-start(bf16[4,320,320]{2,1,0:T(8,128)(2,1)S(1)} %collective-permute-done.36), channel_id=1, source_target_pairs={{0,256},{128,384},{256,0},{384,128},{1,257},{129,385},{257,1},{385... | collective-permute-start | bytes 2457608 | tf_op jit(solution)/shard_map/ppermute | solution.py:26
  (14 other events, 168.9 us)
Sparse Core Ops, SparseCore 0:
  252.7 164.9 all-reduce.6
  420.7 318.3 all-reduce.4
